TPU v7x, 32 devices: a whole 2x2x4 slice. The times are simulated.
32 devices in a mesh: gx: 8 (over z, y), gy: 4 (over x, core).
Axes of the slice: x: 2, y: 2, z: 4, core: 2. Of those that a mesh axis runs over, the one named last changes fastest.
Arguments:
- state: float32 [256, 256, 128], P('gx', 'gy'), may hold values from -6 to 6
- syndromes: int32 [2, 256, 256], P(None, 'gx', 'gy'), may hold values from 0 to 1
- erased: int32 [2, 64, 64], P(None, 'gx', 'gy'), may hold values 0 or 1
- readers: int32 [4096, 1], P(('gx', 'gy')), may hold values from 0 to 31; in each aligned block of 128 rows (0 to 127, 128 to 255, ...) at most 8 rows name the same one
- conv_weight: float32 [9, 128, 128], replicated, may hold values from -0.1875 to 0.1875
- syndrome_table: float32 [2, 128], replicated, may hold values from -6 to 6
- erasure_vector: float32 [128], replicated, may hold values from -6 to 6
- read_weight: float32 [4096, 128], P(('gx', 'gy')), may hold values from -0.5 to 0.5
- erasure_offset: float32 [128], replicated, may hold values from -6 to 6
Outputs:
- final_state: float32 [256, 256, 128], P('gx', 'gy')
Inputs may be any that keep to these rules, and one draw needn't show every extreme that they name: `readers`: among the 128 blocks of one device no reader is named more than 8 times, a bound that some block reaches.
All inputs are finite; a program needn't handle non-finite values. No bound on the sum of `erased` on one device may be relied on, other than what follows from the above.
Results may differ from a plain program's by a relative error of at most 0.0003.
Values sent between devices are 32-bit elements; how exact they have to be, the bound alone decides.
A program may use at most 64 MiB of HBM per device.

v0:
```python
import jax
import jax.numpy as jnp
from jax import lax
from jax.sharding import PartitionSpec as P

BS = 4
ROUNDS = 2


precise = lax.Precision.HIGHEST


def padded_2(cells, sides, width):
    for axis, dim in sides:
        count = lax.axis_size(axis)
        ends = count - 1
        head = lax.slice_in_dim(cells, 0, width, axis=dim)
        tail = lax.slice_in_dim(cells, cells.shape[dim] - width, cells.shape[dim], axis=dim)
        cells = jnp.concatenate(
            [
                lax.ppermute(tail, axis, [(i, (i + 1) % count) for i in range(ends)]),
                cells,
                lax.ppermute(head, axis, [((i + 1) % count, i) for i in range(ends)]),
            ],
            axis=dim,
        )
    return cells


def to_blocks(field, block_side):
    row_count, col_count, channels = field.shape
    block_grid = field.reshape(
        row_count // block_side, block_side, col_count // block_side, block_side, channels
    )
    return block_grid.transpose(0, 2, 1, 3, 4).reshape(
        row_count // block_side * (col_count // block_side), block_side * block_side * channels
    )


def spread_cells(values, block_rows, block_cols, block_side):
    width = values.shape[-1]
    block_grid = values.reshape(block_rows, 1, block_cols, 1, width)
    return jnp.broadcast_to(
        block_grid, (block_rows, block_side, block_cols, block_side, width)
    ).reshape(block_rows * block_side, block_cols * block_side, width)


def reader_head(payload, flag_vals, weight, offset, form):
    channels = offset.shape[0]
    lead_shape = payload.shape[:-1]
    cell_vals = payload.reshape(lead_shape + (payload.shape[-1] // channels, channels))
    mixed_vals = jnp.tanh(jnp.einsum(form, cell_vals, weight, precision=precise))
    pooled = jnp.mean(mixed_vals, axis=-2)
    return jnp.tanh(pooled + flag_vals[..., None] * offset)


def per_device(
    state,
    syndromes,
    erased,
    readers,
    conv_weight,
    syndrome_table,
    erasure_vector,
    read_weight,
    erasure_offset,
):
    tile_rows, tile_cols, channels = state.shape
    block_side = BS
    block_rows = tile_rows // block_side
    block_cols = tile_cols // block_side
    block_count = block_rows * block_cols
    gx_count = lax.axis_size("gx")
    gy_count = lax.axis_size("gy")
    device_count = gx_count * gy_count
    reader_ids = readers[:, 0]
    all_weights = lax.all_gather(read_weight, ("gx", "gy"), axis=0, tiled=True)
    block_weights = all_weights.reshape(device_count, channels, channels)[reader_ids]
    field = state
    for round_index in range(ROUNDS):
        block_flags = erased[round_index].reshape(block_count).astype(jnp.float32)
        block_states = to_blocks(field, block_side)
        corrections = reader_head(
            block_states, block_flags, block_weights, erasure_offset, "bpc,bcd->bpd"
        )
        correction_cells = spread_cells(corrections, block_rows, block_cols, block_side)
        padded = padded_2(field, (("gx", 0), ("gy", 1)), 1)
        conv_sum = jnp.zeros((tile_rows * tile_cols, channels), jnp.float32)
        for tap_index in range(9):
            row_off = tap_index // 3
            col_off = tap_index % 3
            shifted = padded[row_off : row_off + tile_rows, col_off : col_off + tile_cols].reshape(
                -1, channels
            )
            conv_sum = conv_sum + jnp.dot(
                shifted,
                conv_weight[tap_index],
                precision=precise,
                preferred_element_type=jnp.float32,
            )
        conv_sum = conv_sum.reshape(tile_rows, tile_cols, channels)
        erased_cells = spread_cells(
            erased[round_index][:, :, None], block_rows, block_cols, block_side
        )
        bits = syndromes[round_index][:, :, None]
        inputs = jnp.where(
            erased_cells > 0,
            erasure_vector,
            jnp.where(bits == 1, syndrome_table[1], syndrome_table[0]),
        )
        field = 0.5 * field + jnp.tanh(conv_sum + inputs + correction_cells)
    return field


def solution(mesh):
    placed = (
        P("gx", "gy", None),
        P(None, "gx", "gy"),
        P(None, "gx", "gy"),
        P(("gx", "gy"), None),
        P(),
        P(),
        P(),
        P(("gx", "gy"), None),
        P(),
    )
    return jax.shard_map(
        per_device, mesh=mesh, in_specs=placed, out_specs=P("gx", "gy", None), check_vma=False
    )
```

profile of v0, /device:TPU:1, one launch (start us, length us, event | category | flops | bytes accessed | tf_op | source)
XLA Modules:
  0.0 124.9 jit_solution(18058128545281652086)
XLA Ops:
  8.0 1.3 %collective-permute-start.1 = (f32[1,64,128]{2,1,0:T(8,128)S(1)}, f32[1,64,128]{2,1,0:T(8,128)S(1)}, u32[]{:S(2)}, u32[]{:S(2)}) collective-permute-start(f32[1,64,128]{2,1,0:T(8,128)S(1)} %get-tuple-element.33), channel_id=1, source_target_pairs={{4,0},{8,4},{12,8},{16,12},{20,16},{24,20},{28,24},{5,1},{9,5},{13... | collective-permute-start | bytes 98312 | tf_op jit(solution)/shard_map/ppermute | solution.py:23
  9.3 4.6 %collective-permute-start = (f32[1,64,128]{2,1,0:T(8,128)S(1)}, f32[1,64,128]{2,1,0:T(8,128)S(1)}, u32[]{:S(2)}, u32[]{:S(2)}) collective-permute-start(f32[1,64,128]{2,1,0:T(8,128)S(1)} %get-tuple-element.34), channel_id=1, source_target_pairs={{0,4},{4,8},{8,12},{12,16},{16,20},{20,24},{24,28},{1,5},{5,9},{9,... | collective-permute-start | bytes 98312 | tf_op jit(solution)/shard_map/ppermute | solution.py:21
  18.1 1.4 %copy.12 = f32[8,16,4,4,128]{4,3,2,1,0:T(4,128)S(1)} copy(f32[8,16,4,4,128]{4,3,1,2,0:T(4,128)} %bitcast.125) | data formatting | bytes 2097152 | tf_op jit(solution)/shard_map/transpose | solution.py:35
  20.0 4.5 %collective-permute-start.2 = (f32[34,1,128]{2,1,0:T(1,128)S(1)}, f32[34,1,128]{2,1,0:T(1,128)S(1)}, u32[]{:S(2)}, u32[]{:S(2)}) collective-permute-start(f32[34,1,128]{2,1,0:T(1,128)S(1)} %get-tuple-element.24), channel_id=1, source_target_pairs={{0,1},{1,2},{2,3},{4,5},{5,6},{6,7},{8,9},{9,10},{10,11},{12,13},{... | collective-permute-start | bytes 52232 | tf_op jit(solution)/shard_map/ppermute | solution.py:21
  24.4 1.9 %collective-permute-start.3 = (f32[34,1,128]{2,1,0:T(1,128)S(1)}, f32[34,1,128]{2,1,0:T(1,128)S(1)}, u32[]{:S(2)}, u32[]{:S(2)}) collective-permute-start(f32[34,1,128]{2,1,0:T(1,128)S(1)} %get-tuple-element.25), channel_id=1, source_target_pairs={{1,0},{2,1},{3,2},{5,4},{6,5},{7,6},{9,8},{10,9},{11,10},{13,12},{... | collective-permute-start | bytes 52232 | tf_op jit(solution)/shard_map/ppermute | solution.py:23
  28.3 1.1 collective-permute-done.3
  30.4 1.0 fusion.11
  31.4 1.0 convolution_add_fusion.12
  35.4 1.0 convolution_add_fusion.8
  36.3 1.1 fusion.2
  37.4 31.7 %all-gather.2.cloned.1.call-done = f32[4096,128]{1,0:T(8,128)} async-done(((f32[128,128]{1,0:T(8,128)}), f32[4096,128]{1,0:T(8,128)}) %all-gather.2.cloned.1.call-update) | async-done | bytes 2097168 | tf_op jit(solution)/shard_map/all_gather | solution.py:77
  69.1 5.9 %gather_fusion = f32[128,128,128]{2,1,0:T(8,128)} fusion(f32[32,128,128]{2,1,0:T(8,128)} %bitcast.124, s32[1024]{0:T(1024)S(1)} %pad_clamp_fusion), kind=kCustom, calls=%fused_computation | custom fusion | bytes 16777728 | tf_op jit(solution)/shard_map/gather | solution.py:78
  75.1 10.5 %fusion.3 = f32[128,128]{1,0:T(8,128)S(1)} fusion(f32[128,128,128]{2,1,0:T(8,128)} %gather_fusion, f32[128,16,128]{2,1,0:T(8,128)S(1)} %bitcast.132), kind=kOutput, calls=%fused_computation.29 | convolution fusion | flops 402898944 | bytes 9502720 | tf_op jit(solution)/shard_map/bpc,bcd->bpd/dot_general | solution.py:52
  87.0 3.1 %collective-permute-start.4 = (f32[1,64,128]{2,1,0:T(8,128)S(1)}, f32[1,64,128]{2,1,0:T(8,128)S(1)}, u32[]{:S(2)}, u32[]{:S(2)}) collective-permute-start(f32[1,64,128]{2,1,0:T(8,128)S(1)} %get-tuple-element.28), channel_id=1, source_target_pairs={{0,4},{4,8},{8,12},{12,16},{16,20},{20,24},{24,28},{1,5},{5,9},{9,... | collective-permute-start | bytes 98312 | tf_op jit(solution)/shard_map/ppermute | solution.py:21
  90.1 1.3 %collective-permute-start.5 = (f32[1,64,128]{2,1,0:T(8,128)S(1)}, f32[1,64,128]{2,1,0:T(8,128)S(1)}, u32[]{:S(2)}, u32[]{:S(2)}) collective-permute-start(f32[1,64,128]{2,1,0:T(8,128)S(1)} %get-tuple-element.29), channel_id=1, source_target_pairs={{4,0},{8,4},{12,8},{16,12},{20,16},{24,20},{28,24},{5,1},{9,5},{13... | collective-permute-start | bytes 98312 | tf_op jit(solution)/shard_map/ppermute | solution.py:23
  91.6 7.4 %fusion.4 = f32[128,128]{1,0:T(8,128)S(1)} fusion(f32[128,16,128]{2,1,0:T(8,128)S(1)} %bitcast.137, f32[128,128,128]{2,1,0:T(8,128)S(1)} %copy-done), kind=kOutput, calls=%fused_computation.30 | convolution fusion | flops 402898944 | bytes 9502720 | tf_op jit(solution)/shard_map/bpc,bcd->bpd/dot_general | solution.py:52
  99.1 2.8 %collective-permute-start.6 = (f32[34,1,128]{2,1,0:T(1,128)S(1)}, f32[34,1,128]{2,1,0:T(1,128)S(1)}, u32[]{:S(2)}, u32[]{:S(2)}) collective-permute-start(f32[34,1,128]{2,1,0:T(1,128)S(1)} %get-tuple-element.19), channel_id=1, source_target_pairs={{0,1},{1,2},{2,3},{4,5},{5,6},{6,7},{8,9},{9,10},{10,11},{12,13},{... | collective-permute-start | bytes 52232 | tf_op jit(solution)/shard_map/ppermute | solution.py:21
  102.0 2.1 %collective-permute-start.7 = (f32[34,1,128]{2,1,0:T(1,128)S(1)}, f32[34,1,128]{2,1,0:T(1,128)S(1)}, u32[]{:S(2)}, u32[]{:S(2)}) collective-permute-start(f32[34,1,128]{2,1,0:T(1,128)S(1)} %get-tuple-element.20), channel_id=1, source_target_pairs={{1,0},{2,1},{3,2},{5,4},{6,5},{7,6},{9,8},{10,9},{11,10},{13,12},{... | collective-permute-start | bytes 52232 | tf_op jit(solution)/shard_map/ppermute | solution.py:23
  105.3 1.9 %collective-permute-done.7 = f32[34,1,128]{2,1,0:T(1,128)S(1)} collective-permute-done((f32[34,1,128]{2,1,0:T(1,128)S(1)}, f32[34,1,128]{2,1,0:T(1,128)S(1)}, u32[]{:S(2)}, u32[]{:S(2)}) %collective-permute-start.7) | collective-permute-done | bytes 17440 | tf_op jit(solution)/shard_map/ppermute | solution.py:23
  109.2 1.0 convolution_add_fusion.6
  110.2 1.0 convolution_add_fusion.5
  112.2 1.0 convolution_add_fusion.3
  115.2 1.1 fusion
  116.5 1.5 %tanh_add_fusion = f32[32,64,128]{2,1,0:T(8,128)} fusion(f32[32,64,128]{2,1,0:T(8,128)S(1)} %bitcast.134, f32[32,64,128]{2,1,0:T(8,128)S(1)} %bitcast.144, f32[32,64,128]{2,1,0:T(8,128)S(1)} %tanh_add_fusion.1, f32[128]{0:T(128)S(1)} %get-tuple-element.42, f32[128]{0:T(128)S(1)} %get-tuple-element.41, f32[128]{0:T(128)S(1)} %copy-done.5, ...), kind=kLoop, calls=%fused_computation.41 | loop fusion | flops 1572864 | bytes 4199936 | tf_op jit(solution)/shard_map/add | solution.py:111
  (59 shorter events, 19.9 us)
Async XLA Ops:
  6.5 62.6 %all-gather.2.cloned.1.call-start = ((), (), s32[]{:S(2)}) async-start(), calls=%async_computation | async-start | bytes 2162688 | tf_op jit(solution)/shard_map/all_gather | solution.py:77
  8.0 11.6 %collective-permute-start.1 = (f32[1,64,128]{2,1,0:T(8,128)S(1)}, f32[1,64,128]{2,1,0:T(8,128)S(1)}, u32[]{:S(2)}, u32[]{:S(2)}) collective-permute-start(f32[1,64,128]{2,1,0:T(8,128)S(1)} %get-tuple-element.33), channel_id=1, source_target_pairs={{4,0},{8,4},{12,8},{16,12},{20,16},{24,20},{28,24},{5,1},{9,5},{13... | collective-permute-start | bytes 98312 | tf_op jit(solution)/shard_map/ppermute | solution.py:23
  9.3 10.2 %collective-permute-start = (f32[1,64,128]{2,1,0:T(8,128)S(1)}, f32[1,64,128]{2,1,0:T(8,128)S(1)}, u32[]{:S(2)}, u32[]{:S(2)}) collective-permute-start(f32[1,64,128]{2,1,0:T(8,128)S(1)} %get-tuple-element.34), channel_id=1, source_target_pairs={{0,4},{4,8},{8,12},{12,16},{16,20},{20,24},{24,28},{1,5},{5,9},{9,... | collective-permute-start | bytes 98312 | tf_op jit(solution)/shard_map/ppermute | solution.py:21
  14.7 5.0 %copy-start.1 = (f32[32,64,128]{2,1,0:T(8,128)S(1)}, f32[32,64,128]{2,1,0:T(8,128)}, u32[]{:S(2)}) copy-start(f32[32,64,128]{2,1,0:T(8,128)} %param.9) | copy-start | bytes 3145732
  19.6 6.8 %copy-start.2 = (f32[9,128,128]{2,1,0:T(8,128)S(1)}, f32[9,128,128]{2,1,0:T(8,128)}, u32[]{:S(2)}) copy-start(f32[9,128,128]{2,1,0:T(8,128)} %param.13) | copy-start | bytes 1769476
  20.0 8.4 %collective-permute-start.2 = (f32[34,1,128]{2,1,0:T(1,128)S(1)}, f32[34,1,128]{2,1,0:T(1,128)S(1)}, u32[]{:S(2)}, u32[]{:S(2)}) collective-permute-start(f32[34,1,128]{2,1,0:T(1,128)S(1)} %get-tuple-element.24), channel_id=1, source_target_pairs={{0,1},{1,2},{2,3},{4,5},{5,6},{6,7},{8,9},{9,10},{10,11},{12,13},{... | collective-permute-start | bytes 52232 | tf_op jit(solution)/shard_map/ppermute | solution.py:21
  24.4 5.1 %collective-permute-start.3 = (f32[34,1,128]{2,1,0:T(1,128)S(1)}, f32[34,1,128]{2,1,0:T(1,128)S(1)}, u32[]{:S(2)}, u32[]{:S(2)}) collective-permute-start(f32[34,1,128]{2,1,0:T(1,128)S(1)} %get-tuple-element.25), channel_id=1, source_target_pairs={{1,0},{2,1},{3,2},{5,4},{6,5},{7,6},{9,8},{10,9},{11,10},{13,12},{... | collective-permute-start | bytes 52232 | tf_op jit(solution)/shard_map/ppermute | solution.py:23
  75.0 10.6 %copy-start.4 = (f32[128]{0:T(128)S(1)}, f32[128]{0:T(128)}, u32[]{:S(2)}) copy-start(f32[128]{0:T(128)} %param.17) | copy-start | bytes 1540
  75.1 16.5 %copy-start = (f32[128,128,128]{2,1,0:T(8,128)S(1)}, f32[128,128,128]{2,1,0:T(8,128)}, u32[]{:S(2)}) copy-start(f32[128,128,128]{2,1,0:T(8,128)} %gather_fusion) | copy-start | bytes 25165828
  85.6 0.7 copy-start.5
  87.0 12.1 %collective-permute-start.4 = (f32[1,64,128]{2,1,0:T(8,128)S(1)}, f32[1,64,128]{2,1,0:T(8,128)S(1)}, u32[]{:S(2)}, u32[]{:S(2)}) collective-permute-start(f32[1,64,128]{2,1,0:T(8,128)S(1)} %get-tuple-element.28), channel_id=1, source_target_pairs={{0,4},{4,8},{8,12},{12,16},{16,20},{20,24},{24,28},{1,5},{5,9},{9,... | collective-permute-start | bytes 98312 | tf_op jit(solution)/shard_map/ppermute | solution.py:21
  90.1 9.0 %collective-permute-start.5 = (f32[1,64,128]{2,1,0:T(8,128)S(1)}, f32[1,64,128]{2,1,0:T(8,128)S(1)}, u32[]{:S(2)}, u32[]{:S(2)}) collective-permute-start(f32[1,64,128]{2,1,0:T(8,128)S(1)} %get-tuple-element.29), channel_id=1, source_target_pairs={{4,0},{8,4},{12,8},{16,12},{20,16},{24,20},{28,24},{5,1},{9,5},{13... | collective-permute-start | bytes 98312 | tf_op jit(solution)/shard_map/ppermute | solution.py:23
  99.1 6.2 %collective-permute-start.6 = (f32[34,1,128]{2,1,0:T(1,128)S(1)}, f32[34,1,128]{2,1,0:T(1,128)S(1)}, u32[]{:S(2)}, u32[]{:S(2)}) collective-permute-start(f32[34,1,128]{2,1,0:T(1,128)S(1)} %get-tuple-element.19), channel_id=1, source_target_pairs={{0,1},{1,2},{2,3},{4,5},{5,6},{6,7},{8,9},{9,10},{10,11},{12,13},{... | collective-permute-start | bytes 52232 | tf_op jit(solution)/shard_map/ppermute | solution.py:21
  102.0 2.3 %copy-start.3 = (f32[9,128,128]{2,1,0:T(8,128)S(1)}, f32[9,128,128]{2,1,0:T(8,128)}, u32[]{:S(2)}) copy-start(f32[9,128,128]{2,1,0:T(8,128)} %param.13) | copy-start | bytes 1769476
  102.0 5.2 %collective-permute-start.7 = (f32[34,1,128]{2,1,0:T(1,128)S(1)}, f32[34,1,128]{2,1,0:T(1,128)S(1)}, u32[]{:S(2)}, u32[]{:S(2)}) collective-permute-start(f32[34,1,128]{2,1,0:T(1,128)S(1)} %get-tuple-element.20), channel_id=1, source_target_pairs={{1,0},{2,1},{3,2},{5,4},{6,5},{7,6},{9,8},{10,9},{11,10},{13,12},{... | collective-permute-start | bytes 52232 | tf_op jit(solution)/shard_map/ppermute | solution.py:23
Sparse Core Ops, SparseCore 0:
  10.2 58.8 all-gather.1
where the time goes:
time: 127 us; the launch traced here: 125 us
  matrix products  35.7 us (28%)
  waiting for transfers between devices  35.5 us (28%)
  starting transfers between devices  21.5 us (17%)
  between operations  13.9 us (11%)
  local copies, waits for them, and re-layouts  11.2 us (9%)
  other arithmetic  7.04 us (6%)
    all_gather x1, waiting for transfers between devices, per_device(): all_weights = lax.all_gather(read_weight, ('gx', 'gy'), axis=0, tiled=True)  31.7 us
    dot_general x2, matrix products, reader_head(): jnp.einsum(form, cell_vals, weight, precision=precise)  17.9 us
    dot_general x18, matrix products, per_device(): jnp.dot(shifted, conv_weight[tap_index], precision=precise, preferred_ele...  17.8 us
    ppermute x4, starting transfers between devices, padded_2(): lax.ppermute(tail, axis, [(i, (i + 1) % count) for i in range(ends)])  15 us
    ppermute x4, starting transfers between devices, padded_2(): lax.ppermute(head, axis, [((i + 1) % count, i) for i in range(ends)])  6.54 us
    gather x1, local copies, waits for them, and re-layouts, per_device(): all_weights.reshape(device_count, channels, channels)[reader_ids]  5.92 us
    ppermute x4, waiting for transfers between devices, padded_2(): lax.ppermute(head, axis, [((i + 1) % count, i) for i in range(ends)])  3.03 us
  transfers between devices with their start and end apart: 9, of which 3 were waited for; matrix products, arithmetic and copies ran while one was open for 20% of the time, Pallas kernels for 0%

commit v1 on v0

v1 whole, which is shorter than its diff:
```python
import functools

import jax
import jax.numpy as jnp
from jax import lax
from jax.experimental import pallas as pl
from jax.experimental.pallas import tpu as pltpu
from jax.sharding import PartitionSpec as P

MESH = pl.DeviceIdType.MESH
BS = 4
ROUNDS = 2
SLOTS = 8
LEFT = 8
ORDERS = (("z", "y", "x", 0, 64), ("z", "x", "y", 64, 128))
SIDES = ((-1, 0), (1, 0), (0, -1), (0, 1), (-1, -1), (-1, 1), (1, -1), (1, 1))
F32 = jnp.float32
BF16 = jnp.bfloat16


def split_2(values):
    high = values.astype(BF16)
    return high, (values - high.astype(F32)).astype(BF16)


def split_3(values):
    high, rest = values.astype(BF16).astype(F32), values
    rest = rest - high
    mid = rest.astype(BF16).astype(F32)
    return high, mid, rest - mid


def kernel(
    sizes,
    state_ref,
    syn_ref,
    er_ref,
    readers_ref,
    conv_ref,
    table_ref,
    vector_ref,
    read_ref,
    offset_ref,
    out_ref,
    weights,
    padded,
    taps_high,
    taps_low,
    conv_both,
    conv_sum,
    cells,
    sorted_cells,
    pooled,
    pick,
    place,
    spread,
    row_out,
    col_out,
    row_in,
    col_in,
    corner_out,
    corner_in,
    send_sem,
    recv_sem,
    core_send,
    core_recv,
    halo_send,
    halo_recv,
):
    nz, ny, nx = sizes
    lengths = {"z": nz, "y": ny, "x": nx}
    rows, cols, chan = state_ref.shape
    block_rows, block_cols = rows // BS, cols // BS
    blocks = block_rows * block_cols
    slots = nz * ny * nx * 2 * SLOTS
    gx, gy = lax.axis_index("gx"), lax.axis_index("gy")
    at = {"z": gx // ny, "y": gx % ny, "x": gy // 2}
    core = gy % 2
    gx_count, gy_count = nz * ny, nx * 2

    def device(place_of, c):
        return (place_of["z"] * ny + place_of["y"], place_of["x"] * 2 + c)

    def held(order, wave, place_of, c):
        full = order[:wave]
        idx = [pl.ds(0, lengths[d]) if d in full else place_of[d] for d in "zyx"]
        return weights.at[idx[0], idx[1], idx[2], c, pl.ds(order[3], order[4] - order[3]), :]

    def shifted(dim, k):
        moved = dict(at)
        moved[dim] = (at[dim] + k + lengths[dim]) % lengths[dim]
        return moved

    def wave_copies(wave):
        made = []
        n = 0
        for order in ORDERS:
            dim = order[wave]
            for k in range(1, lengths[dim]):
                other, source = shifted(dim, k), shifted(dim, -k)
                mine, theirs = held(order, wave, at, core), held(order, wave, source, core)
                passed = held(order, wave, source, 1 - core)
                out = pltpu.make_async_remote_copy(
                    mine, mine, send_sem.at[wave, n], recv_sem.at[wave, n],
                    device_id=device(other, core), device_id_type=MESH)
                arriving = pltpu.make_async_remote_copy(
                    theirs, theirs, send_sem.at[wave, n], recv_sem.at[wave, n],
                    device_id=device(other, core), device_id_type=MESH)
                on = pltpu.make_async_remote_copy(
                    theirs, theirs, core_send.at[wave, n], core_recv.at[wave, n],
                    device_id=device(at, 1 - core), device_id_type=MESH)
                back = pltpu.make_async_remote_copy(
                    passed, passed, core_send.at[wave, n], core_recv.at[wave, n],
                    device_id=device(at, 1 - core), device_id_type=MESH)
                made.append((out, arriving, on, back))
                n += 1
        return made

    def own_pair():
        made = []
        for c in (core, 1 - core):
            part = weights.at[at["z"], at["y"], at["x"], c]
            made.append(pltpu.make_async_remote_copy(
                part, part, core_send.at[3, 0], core_recv.at[3, 0],
                device_id=device(at, 1 - core), device_id_type=MESH))
        return made

    waves = [wave_copies(w) for w in range(3)]
    own_out, own_in = own_pair()

    there = []
    for dr, dc in SIDES:
        ok = jnp.bool_(True)
        if dr:
            ok = (gx + dr >= 0) & (gx + dr < gx_count)
        if dc:
            more = (gy + dc >= 0) & (gy + dc < gy_count)
            ok = more if not dr else ok & more
        there.append(ok)

    def halo_refs(r, side):
        dr, dc = SIDES[side]
        if side < 2:
            return row_out.at[r, side], row_in.at[r, side]
        if side < 4:
            return col_out.at[r, side - 2], col_in.at[r, side - 2]
        return corner_out.at[r, side - 4], corner_in.at[r, side - 4]

    opposite = (1, 0, 3, 2, 7, 6, 5, 4)

    def halo_copy(r, side):
        dr, dc = SIDES[side]
        src, _ = halo_refs(r, side)
        _, dst = halo_refs(r, opposite[side])
        return pltpu.make_async_remote_copy(
            src, dst, halo_send.at[r, side], halo_recv.at[r, opposite[side]],
            device_id=(gx + dr, gy + dc), device_id_type=MESH)

    def halo_arrival(r, side):
        dr, dc = SIDES[side]
        _, dst = halo_refs(r, side)
        return pltpu.make_async_remote_copy(
            dst, dst, halo_send.at[r, side], halo_recv.at[r, side],
            device_id=(gx + dr, gy + dc), device_id_type=MESH)

    def for_sides(do):
        for side in range(8):
            pl.when(there[side])(functools.partial(do, side))

    def pack_borders(r):
        row_out[r, 0] = padded[1, LEFT:LEFT + cols, :]
        row_out[r, 1] = padded[rows, LEFT:LEFT + cols, :]

        def one(i, _):
            col_out[r, 0, pl.ds(i, 1), :] = padded[1 + i, LEFT:LEFT + 1, :]
            col_out[r, 1, pl.ds(i, 1), :] = padded[1 + i, LEFT + cols - 1:LEFT + cols, :]
            return 0

        lax.fori_loop(0, rows, one, 0, unroll=4)
        for n, (dr, dc) in enumerate(SIDES[4:]):
            line = 1 if dr < 0 else rows
            col = LEFT if dc < 0 else LEFT + cols - 1
            corner_out[r, n] = jnp.broadcast_to(padded[line, col:col + 1, :], (8, chan))

    def place_borders(r):
        padded[0, LEFT:LEFT + cols, :] = row_in[r, 0]
        padded[rows + 1, LEFT:LEFT + cols, :] = row_in[r, 1]

        def one(i, _):
            padded[1 + i, LEFT - 1:LEFT, :] = col_in[r, 0, pl.ds(i, 1), :]
            padded[1 + i, LEFT + cols:LEFT + cols + 1, :] = col_in[r, 1, pl.ds(i, 1), :]
            return 0

        lax.fori_loop(0, rows, one, 0, unroll=4)
        for n, (dr, dc) in enumerate(SIDES[4:]):
            line = 0 if dr < 0 else rows + 1
            col = LEFT - 1 if dc < 0 else LEFT + cols
            padded[line, col:col + 1, :] = corner_in[r, n, 0:1, :]

    weights[at["z"], at["y"], at["x"], core] = read_ref[...]

    def fill(i, _):
        padded[1 + i, LEFT:LEFT + cols, :] = state_ref[i]
        return 0

    lax.fori_loop(0, rows, fill, 0, unroll=2)
    pack_borders(0)

    def clear(side):
        for r in range(ROUNDS):
            _, dst = halo_refs(r, side)
            dst[...] = jnp.zeros(dst.shape, F32)

    for side in range(8):
        pl.when(jnp.logical_not(there[side]))(functools.partial(clear, side))

    barrier = pltpu.get_barrier_semaphore()
    count = jnp.int32(1)
    pl.semaphore_signal(barrier, inc=1, device_id=device(at, 1 - core), device_id_type=MESH)
    for dim in "zyx":
        for k in range(1, lengths[dim]):
            pl.semaphore_signal(barrier, inc=1, device_id=device(shifted(dim, k), core), device_id_type=MESH)
            count = count + 1

    def greet(side):
        dr, dc = SIDES[side]
        pl.semaphore_signal(barrier, inc=1, device_id=(gx + dr, gy + dc), device_id_type=MESH)

    for_sides(greet)
    for side in range(8):
        count = count + there[side].astype(jnp.int32)
    pl.semaphore_wait(barrier, count)

    for out, _, _, _ in waves[0]:
        out.start()
    own_out.start()
    for_sides(lambda side: halo_copy(0, side).start())

    def next_wave(wave):
        for _, arriving, _, _ in waves[wave]:
            arriving.wait_recv()
        if wave + 1 < 3:
            for out, _, _, _ in waves[wave + 1]:
                out.start()
        for _, _, on, _ in waves[wave]:
            on.start()

    first = lax.broadcasted_iota(jnp.int32, (blocks, blocks), 0)
    second = lax.broadcasted_iota(jnp.int32, (blocks, blocks), 1)
    down = jnp.broadcast_to(readers_ref[...].astype(F32), (blocks, blocks))
    across = jnp.sum(jnp.where(first == second, down, 0.0), axis=0, keepdims=True)
    same = jnp.where(down == across, 1.0, 0.0)
    slot_across = SLOTS * across + jnp.sum(jnp.where(first < second, same, 0.0), axis=0, keepdims=True)
    slot_down = SLOTS * down[:, 0:1] + jnp.sum(jnp.where(second < first, same, 0.0), axis=1, keepdims=True)
    slot_at = lax.broadcasted_iota(jnp.int32, (slots, blocks), 0).astype(F32)
    pick[...] = jnp.where(slot_at == slot_across, 1.0, 0.0).astype(BF16)
    slot_at = lax.broadcasted_iota(jnp.int32, (blocks, slots), 1).astype(F32)
    place[...] = jnp.where(slot_at == slot_down, 1.0, 0.0).astype(BF16)

    line = lax.broadcasted_iota(jnp.int32, (16, chan), 0)
    embed = jnp.zeros((16, chan), F32)
    for n, row in enumerate((vector_ref[...], table_ref[1:2, :], table_ref[0:1, :])):
        for m, part in enumerate(split_3(row)):
            embed = jnp.where(line == 3 * n + m, part, embed)
    embed = embed.astype(BF16)
    feature = lax.broadcasted_iota(jnp.int32, (16, cols), 0)

    def split_conv(t, _):
        high, low = split_2(conv_ref[t])
        conv_both[pl.ds(t * chan, chan), 0:chan] = high
        conv_both[pl.ds(t * chan, chan), chan:2 * chan] = low
        return 0

    lax.fori_loop(0, 9, split_conv, 0)

    def build_cells():
        def one(b, _):
            for i in range(BS):
                for q in range(BS):
                    high, low = split_2(padded[1 + BS * b + i, pl.ds(LEFT + q, block_cols, stride=BS), :])
                    cells[i * BS + q, pl.ds(b * block_cols, block_cols), 0:chan] = high
                    cells[i * BS + q, pl.ds(b * block_cols, block_cols), chan:2 * chan] = low
            return 0

        lax.fori_loop(0, block_rows, one, 0)

        def sort(p, _):
            sorted_cells[p] = jnp.dot(pick[...], cells[p], preferred_element_type=F32)
            return 0

        lax.fori_loop(0, BS * BS, sort, 0)

    def build_taps():
        def one(i, _):
            for s in range(3):
                high, low = split_2(padded[i, LEFT - 1 + s:LEFT - 1 + s + cols, :])
                taps_high[i, :, s * chan:(s + 1) * chan] = high
                taps_low[i, :, s * chan:(s + 1) * chan] = low
            return 0

        lax.fori_loop(0, rows + 2, one, 0, unroll=2)

    def convolve():
        step = 8

        def one(n, _):
            def lines(ref):
                parts = [ref[pl.ds(n * step + a, step)].reshape(step * cols, 3 * chan) for a in range(3)]
                return jnp.concatenate(parts, axis=1)

            both = jnp.dot(lines(taps_high), conv_both[...], preferred_element_type=F32)
            low = jnp.dot(lines(taps_low), conv_both[:, 0:chan], preferred_element_type=F32)
            total = both[:, 0:chan] + (both[:, chan:] + low)
            conv_sum[pl.ds(n * step, step)] = total.reshape(step, cols, chan)
            return 0

        lax.fori_loop(0, rows // step, one, 0)

    def read_out(r):
        def one(k, _):
            c, x = k % 2, k // 2 % nx
            z, y = k // (2 * nx * ny), k // (2 * nx) % ny
            high, low = split_2(weights[z, y, x, c])
            side = jnp.concatenate([high, low], axis=1)
            weight = jnp.concatenate([side, side], axis=0)
            vals = sorted_cells[:, pl.ds(pl.multiple_of(k * SLOTS, SLOTS), SLOTS), :]
            vals = vals.reshape(BS * BS * SLOTS, 2 * chan).astype(BF16)
            both = jnp.dot(vals, weight, preferred_element_type=F32)
            mixed = jnp.tanh(both[:, 0:chan] + both[:, chan:])
            mean = jnp.sum(mixed.reshape(BS * BS, SLOTS, chan), axis=0) * (1.0 / (BS * BS))
            pooled[pl.ds(pl.multiple_of(k * SLOTS, SLOTS), SLOTS), :] = mean
            return 0

        lax.fori_loop(0, nz * ny * nx * 2, one, 0, unroll=4)
        high, low = split_2(pooled[...])
        both = jnp.dot(place[...], jnp.concatenate([high, low], axis=1), preferred_element_type=F32)
        mean = both[:, 0:chan] + both[:, chan:]
        lane = lax.broadcasted_iota(jnp.int32, (block_cols, block_cols), 1)
        deep = lax.broadcasted_iota(jnp.int32, (block_cols, block_cols), 0)
        flags = er_ref[r].astype(F32)
        for b in range(block_rows):
            flag = jnp.sum(jnp.where(lane == deep, flags[b:b + 1, :], 0.0), axis=1, keepdims=True)
            part = jnp.tanh(mean[b * block_cols:(b + 1) * block_cols] + flag * offset_ref[...])
            for q in range(BS):
                spread[b, pl.ds(q, block_cols, stride=BS), :] = part

    def combine(r, last):
        wide = jnp.where(
            lax.broadcasted_iota(jnp.int32, (block_cols, cols), 1) // BS
            == lax.broadcasted_iota(jnp.int32, (block_cols, cols), 0), 1.0, 0.0).astype(BF16)
        flag_lanes = jnp.dot(er_ref[r].astype(F32).astype(BF16), wide, preferred_element_type=F32)
        bits_all = syn_ref[r].astype(F32)
        for b in range(block_rows):
            gone = flag_lanes[b:b + 1, :]
            for i in range(b * BS, (b + 1) * BS):
                bits = bits_all[i:i + 1, :]
                one_hot = jnp.where(
                    feature < 3, gone,
                    jnp.where(feature < 6, (1.0 - gone) * bits, (1.0 - gone) * (1.0 - bits))).astype(BF16)
                inputs = lax.dot_general(
                    one_hot, embed, (((0,), (0,)), ((), ())), preferred_element_type=F32)
                old = padded[1 + i, LEFT:LEFT + cols, :]
                new = 0.5 * old + jnp.tanh(conv_sum[i] + inputs + spread[b])
                if last:
                    out_ref[i] = new
                else:
                    padded[1 + i, LEFT:LEFT + cols, :] = new

    build_cells()
    for_sides(lambda side: halo_arrival(0, side).wait_recv())
    place_borders(0)
    build_taps()
    next_wave(0)
    convolve()
    next_wave(1)
    next_wave(2)
    for wave in range(3):
        for _, _, _, back in waves[wave]:
            back.wait_recv()
    own_in.wait_recv()
    read_out(0)
    combine(0, False)
    pack_borders(1)
    for_sides(lambda side: halo_copy(1, side).start())
    build_cells()
    read_out(1)
    for_sides(lambda side: halo_arrival(1, side).wait_recv())
    place_borders(1)
    build_taps()
    convolve()
    combine(1, True)

    for wave in range(3):
        for out, _, on, _ in waves[wave]:
            out.wait_send()
            on.wait_send()
    own_out.wait_send()
    for r in range(ROUNDS):
        for_sides(lambda side: halo_copy(r, side).wait_send())


def solution(mesh):
    gx_count, gy_count = mesh.shape["gx"], mesh.shape["gy"]
    nx = gy_count // 2
    ny = nx
    nz = gx_count // ny
    copies = 2 * max(nz - 1, ny - 1, nx - 1)

    def per_device(state, syndromes, erased, readers, conv, table, vector, read, offset):
        rows, cols, chan = state.shape
        blocks = readers.shape[0]
        slots = gx_count * gy_count * SLOTS
        vmem = pltpu.VMEM
        dma = pltpu.SemaphoreType.DMA
        return pl.pallas_call(
            functools.partial(kernel, (nz, ny, nx)),
            out_shape=jax.ShapeDtypeStruct(state.shape, F32),
            in_specs=[pl.BlockSpec(memory_space=vmem)] * 9,
            out_specs=pl.BlockSpec(memory_space=vmem),
            scratch_shapes=[
                vmem((nz, ny, nx, 2, chan, chan), F32),
                vmem((rows + 2, cols + 16, chan), F32),
                vmem((rows + 2, cols, 3 * chan), BF16),
                vmem((rows + 2, cols, 3 * chan), BF16),
                vmem((9 * chan, 2 * chan), BF16),
                vmem((rows, cols, chan), F32),
                vmem((BS * BS, blocks, 2 * chan), BF16),
                vmem((BS * BS, slots, 2 * chan), F32),
                vmem((slots, chan), F32),
                vmem((slots, blocks), BF16),
                vmem((blocks, slots), BF16),
                vmem((rows // BS, cols, chan), F32),
                vmem((ROUNDS, 2, cols, chan), F32),
                vmem((ROUNDS, 2, rows, chan), F32),
                vmem((ROUNDS, 2, cols, chan), F32),
                vmem((ROUNDS, 2, rows, chan), F32),
                vmem((ROUNDS, 4, 8, chan), F32),
                vmem((ROUNDS, 4, 8, chan), F32),
                dma((3, copies)),
                dma((3, copies)),
                dma((4, copies)),
                dma((4, copies)),
                dma((ROUNDS, 8)),
                dma((ROUNDS, 8)),
            ],
            compiler_params=pltpu.CompilerParams(
                collective_id=0, has_side_effects=True, vmem_limit_bytes=56 * 2**20
            ),
        )(state, syndromes, erased, readers, conv, table, vector.reshape(1, -1), read, offset.reshape(1, -1))

    placed = (
        P("gx", "gy", None),
        P(None, "gx", "gy"),
        P(None, "gx", "gy"),
        P(("gx", "gy"), None),
        P(),
        P(),
        P(),
        P(("gx", "gy"), None),
        P(),
    )
    return jax.shard_map(
        per_device, mesh=mesh, in_specs=placed, out_specs=P("gx", "gy", None), check_vma=False
    )
```

time: 127 us -> 46.6 us (0.37); the launches traced: 125 us -> 46 us
  Pallas kernels: 0 us -> 42.3 us
  matrix products: 35.7 us -> 0 us
  waiting for transfers between devices: 35.5 us -> 0 us
  starting transfers between devices: 21.5 us -> 0 us
  between operations: 13.9 us -> 0.01 us
  local copies, waits for them, and re-layouts: 11.2 us -> 3.7 us
  other arithmetic: 7.04 us -> 0 us
    pallas_call x0 -> x1, Pallas kernels: none -> 42.3 us  [per_device(): pl.pallas_call(functools.partial(kernel, (nz, ny, nx)), out_shape=jax.Sha...]
    dot_general x20 -> x0, matrix products: 35.7 us -> none  [the longest x2 17.9 us: reader_head(): jnp.einsum(form, cell_vals, weight, precision=precise)]
    all_gather x1 -> x0, waiting for transfers between devices: 31.7 us -> none  [per_device(): all_weights = lax.all_gather(read_weight, ('gx', 'gy'), axis=0, tiled=True)]
    ppermute x8 -> x0, starting transfers between devices: 21.5 us -> none  [the longest x4 15 us: padded_2(): lax.ppermute(tail, axis, [(i, (i + 1) % count) for i in range(ends)])]
    gather x1 -> x0, local copies, waits for them, and re-layouts: 5.92 us -> none  [per_device(): all_weights.reshape(device_count, channels, channels)[reader_ids]]
    unnamed x13 -> x4, local copies, waits for them, and re-layouts: 0.31 us -> 3.7 us
    ppermute x8 -> x0, waiting for transfers between devices: 3.04 us -> none  [the longest x4 3.03 us: padded_2(): lax.ppermute(head, axis, [((i + 1) % count, i) for i in range(ends)])]
    add x2 -> x0, other arithmetic: 2.25 us -> none  [per_device(): field = 0.5 * field + jnp.tanh(conv_sum + inputs + correction_cells)]
  transfers between devices with their start and end apart: 9 -> 0, of which waited for: 3 -> 0; matrix products, arithmetic and copies ran while one was open for 20% -> 0% of each run, Pallas kernels for 0% -> 0%
where the time goes in v1:
time: 46.6 us; the launch traced here: 46 us
  Pallas kernels  42.3 us (91%)
  local copies, waits for them, and re-layouts  3.7 us (8%)
    pallas_call x1, Pallas kernels, per_device(): pl.pallas_call(functools.partial(kernel, (nz, ny, nx)), out_shape=jax.Sha...  42.3 us
    unnamed x4, local copies, waits for them, and re-layouts  3.7 us

profile of v1, /device:TPU:1, one launch (start us, length us, event | category | flops | bytes accessed | tf_op | source)
XLA Modules:
  0.0 46.0 jit_solution(1048976185419290470)
XLA Ops:
  0.0 0.0 copy-start
  0.0 0.7 %copy-done = s32[128,1]{0,1:T(1,128)S(1)} copy-done((s32[128,1]{0,1:T(1,128)S(1)}, s32[128,1]{0,1:T(1,128)}, u32[]{:S(2)}) %copy-start) | copy-done | bytes 536
  0.7 0.7 %copy.10.readers_ref = s32[128,1]{1,0:T(8,128)} copy(s32[128,1]{0,1:T(1,128)S(1)} %copy-done) | data formatting | bytes 1024 | tf_op args[3]
  1.4 42.3 %shard_map.91 = f32[32,64,128]{2,1,0:T(8,128)} custom-call(f32[32,64,128]{2,1,0:T(8,128)} %state_ref.1, s32[2,32,64]{2,1,0:T(8,128)} %syn_ref.1, s32[2,8,16]{2,1,0:T(8,128)} %er_ref.1, s32[128,1]{1,0:T(8,128)} %copy.10.readers_ref, f32[9,128,128]{2,1,0:T(8,128)} %conv_ref.1, f32[2,128]{1,0:T(2,128)} %table_ref.1, f32[1,128]{1,0:T(1,128)} %bitcast.2, ...), custom_call_target="tpu_custom_call" | custom-call | tf_op jit(solution)/shard_map/pallas_call | solution.py:415
  43.7 2.3 %copy.12 = f32[32,64,128]{2,1,0:T(8,128)} copy(f32[32,64,128]{2,1,0:T(8,128)} %shard_map.91) | data formatting | bytes 2097152
Async XLA Ops:
  0.0 0.7 %copy-start = (s32[128,1]{0,1:T(1,128)S(1)}, s32[128,1]{0,1:T(1,128)}, u32[]{:S(2)}) copy-start(s32[128,1]{0,1:T(1,128)} %param.12) | copy-start | bytes 1540

commit v2 on v1

--- a/solution.py
+++ b/solution.py
@@ -12,7 +12,13 @@
 ROUNDS = 2
 SLOTS = 8
 LEFT = 8
-ORDERS = (("z", "y", "x", 0, 64), ("z", "x", "y", 64, 128))
+ORDERS = (
+    ("z", "y", "x", 0, 40),
+    ("z", "x", "y", 40, 80),
+    ("x", "z", "y", 80, 104),
+    ("y", "z", "x", 104, 128),
+)
+STEP = 8
 SIDES = ((-1, 0), (1, 0), (0, -1), (0, 1), (-1, -1), (-1, 1), (1, -1), (1, 1))
 F32 = jnp.float32
 BF16 = jnp.bfloat16
@@ -60,6 +66,9 @@
     col_in,
     corner_out,
     corner_in,
+    conv_whole,
+    inputs,
+    local_sem,
     send_sem,
     recv_sem,
     core_send,
@@ -69,7 +78,7 @@
 ):
     nz, ny, nx = sizes
     lengths = {"z": nz, "y": ny, "x": nx}
-    rows, cols, chan = state_ref.shape
+    rows, cols, chan = conv_sum.shape
     block_rows, block_cols = rows // BS, cols // BS
     blocks = block_rows * block_cols
     slots = nz * ny * nx * 2 * SLOTS
@@ -91,29 +100,24 @@
         moved[dim] = (at[dim] + k + lengths[dim]) % lengths[dim]
         return moved
 
-    def wave_copies(wave):
+    def wave_copies(o, wave):
         made = []
-        n = 0
-        for order in ORDERS:
-            dim = order[wave]
-            for k in range(1, lengths[dim]):
-                other, source = shifted(dim, k), shifted(dim, -k)
-                mine, theirs = held(order, wave, at, core), held(order, wave, source, core)
-                passed = held(order, wave, source, 1 - core)
-                out = pltpu.make_async_remote_copy(
-                    mine, mine, send_sem.at[wave, n], recv_sem.at[wave, n],
-                    device_id=device(other, core), device_id_type=MESH)
-                arriving = pltpu.make_async_remote_copy(
-                    theirs, theirs, send_sem.at[wave, n], recv_sem.at[wave, n],
-                    device_id=device(other, core), device_id_type=MESH)
-                on = pltpu.make_async_remote_copy(
-                    theirs, theirs, core_send.at[wave, n], core_recv.at[wave, n],
-                    device_id=device(at, 1 - core), device_id_type=MESH)
-                back = pltpu.make_async_remote_copy(
-                    passed, passed, core_send.at[wave, n], core_recv.at[wave, n],
-                    device_id=device(at, 1 - core), device_id_type=MESH)
-                made.append((out, arriving, on, back))
-                n += 1
+        order = ORDERS[o]
+        dim = order[wave]
+        for k in range(1, lengths[dim]):
+            other, source = shifted(dim, k), shifted(dim, -k)
+            mine, theirs = held(order, wave, at, core), held(order, wave, source, core)
+            passed = held(order, wave, source, 1 - core)
+            made.append(tuple(
+                pltpu.make_async_remote_copy(
+                    part, part, sems[0].at[wave, o, k - 1], sems[1].at[wave, o, k - 1],
+                    device_id=target, device_id_type=MESH)
+                for part, sems, target in (
+                    (mine, (send_sem, recv_sem), device(other, core)),
+                    (theirs, (send_sem, recv_sem), device(other, core)),
+                    (theirs, (core_send, core_recv), device(at, 1 - core)),
+                    (passed, (core_send, core_recv), device(at, 1 - core)),
+                )))
         return made
 
     def own_pair():
@@ -121,11 +125,11 @@
         for c in (core, 1 - core):
             part = weights.at[at["z"], at["y"], at["x"], c]
             made.append(pltpu.make_async_remote_copy(
-                part, part, core_send.at[3, 0], core_recv.at[3, 0],
+                part, part, core_send.at[3, 0, 0], core_recv.at[3, 0, 0],
                 device_id=device(at, 1 - core), device_id_type=MESH))
         return made
 
-    waves = [wave_copies(w) for w in range(3)]
+    waves = [[wave_copies(o, w) for w in range(3)] for o in range(len(ORDERS))]
     own_out, own_in = own_pair()
 
     there = []
@@ -197,23 +201,6 @@
             col = LEFT - 1 if dc < 0 else LEFT + cols
             padded[line, col:col + 1, :] = corner_in[r, n, 0:1, :]
 
-    weights[at["z"], at["y"], at["x"], core] = read_ref[...]
-
-    def fill(i, _):
-        padded[1 + i, LEFT:LEFT + cols, :] = state_ref[i]
-        return 0
-
-    lax.fori_loop(0, rows, fill, 0, unroll=2)
-    pack_borders(0)
-
-    def clear(side):
-        for r in range(ROUNDS):
-            _, dst = halo_refs(r, side)
-            dst[...] = jnp.zeros(dst.shape, F32)
-
-    for side in range(8):
-        pl.when(jnp.logical_not(there[side]))(functools.partial(clear, side))
-
     barrier = pltpu.get_barrier_semaphore()
     count = jnp.int32(1)
     pl.semaphore_signal(barrier, inc=1, device_id=device(at, 1 - core), device_id_type=MESH)
@@ -229,29 +216,50 @@
     for_sides(greet)
     for side in range(8):
         count = count + there[side].astype(jnp.int32)
+
+    load_read = pltpu.make_async_copy(read_ref, weights.at[at["z"], at["y"], at["x"], core], local_sem.at[0])
+    load_state = pltpu.make_async_copy(
+        state_ref, padded.at[pl.ds(1, rows), pl.ds(LEFT, cols), :], local_sem.at[1])
+    load_conv = pltpu.make_async_copy(conv_ref, conv_whole, local_sem.at[2])
+    load_read.start()
+    load_state.start()
+    load_conv.start()
+
+    def clear(side):
+        for r in range(ROUNDS):
+            _, dst = halo_refs(r, side)
+            dst[...] = jnp.zeros(dst.shape, F32)
+
+    for side in range(8):
+        pl.when(jnp.logical_not(there[side]))(functools.partial(clear, side))
+    load_read.wait()
+    load_state.wait()
+    pack_borders(0)
     pl.semaphore_wait(barrier, count)
 
-    for out, _, _, _ in waves[0]:
-        out.start()
+    for_sides(lambda side: halo_copy(0, side).start())
+    for order in waves:
+        for out, _, _, _ in order[0]:
+            out.start()
     own_out.start()
-    for_sides(lambda side: halo_copy(0, side).start())
 
     def next_wave(wave):
-        for _, arriving, _, _ in waves[wave]:
-            arriving.wait_recv()
-        if wave + 1 < 3:
-            for out, _, _, _ in waves[wave + 1]:
-                out.start()
-        for _, _, on, _ in waves[wave]:
-            on.start()
+        for order in waves:
+            for _, arriving, _, _ in order[wave]:
+                arriving.wait_recv()
+            if wave + 1 < 3:
+                for out, _, _, _ in order[wave + 1]:
+                    out.start()
+            for _, _, on, _ in order[wave]:
+                on.start()
 
     first = lax.broadcasted_iota(jnp.int32, (blocks, blocks), 0)
     second = lax.broadcasted_iota(jnp.int32, (blocks, blocks), 1)
-    down = jnp.broadcast_to(readers_ref[...].astype(F32), (blocks, blocks))
-    across = jnp.sum(jnp.where(first == second, down, 0.0), axis=0, keepdims=True)
+    across = readers_ref[...].astype(F32)
+    down = jnp.sum(jnp.where(first == second, across, 0.0), axis=1, keepdims=True)
     same = jnp.where(down == across, 1.0, 0.0)
     slot_across = SLOTS * across + jnp.sum(jnp.where(first < second, same, 0.0), axis=0, keepdims=True)
-    slot_down = SLOTS * down[:, 0:1] + jnp.sum(jnp.where(second < first, same, 0.0), axis=1, keepdims=True)
+    slot_down = SLOTS * down + jnp.sum(jnp.where(second < first, same, 0.0), axis=1, keepdims=True)
     slot_at = lax.broadcasted_iota(jnp.int32, (slots, blocks), 0).astype(F32)
     pick[...] = jnp.where(slot_at == slot_across, 1.0, 0.0).astype(BF16)
     slot_at = lax.broadcasted_iota(jnp.int32, (blocks, slots), 1).astype(F32)
@@ -266,11 +274,12 @@
     feature = lax.broadcasted_iota(jnp.int32, (16, cols), 0)
 
     def split_conv(t, _):
-        high, low = split_2(conv_ref[t])
+        high, low = split_2(conv_whole[t])
         conv_both[pl.ds(t * chan, chan), 0:chan] = high
         conv_both[pl.ds(t * chan, chan), chan:2 * chan] = low
         return 0
 
+    load_conv.wait()
     lax.fori_loop(0, 9, split_conv, 0)
 
     def build_cells():
@@ -300,21 +309,22 @@
 
         lax.fori_loop(0, rows + 2, one, 0, unroll=2)
 
-    def convolve():
-        step = 8
-
+    def convolve(n):
+        def lines(ref):
+            parts = [ref[pl.ds(n * STEP + a, STEP)].reshape(STEP * cols, 3 * chan) for a in range(3)]
+            return jnp.concatenate(parts, axis=1)
+
+        both = jnp.dot(lines(taps_high), conv_both[...], preferred_element_type=F32)
+        low = jnp.dot(lines(taps_low), conv_both[:, 0:chan], preferred_element_type=F32)
+        total = both[:, 0:chan] + (both[:, chan:] + low)
+        return total.reshape(STEP, cols, chan)
+
+    def convolve_lines(start, stop):
         def one(n, _):
-            def lines(ref):
-                parts = [ref[pl.ds(n * step + a, step)].reshape(step * cols, 3 * chan) for a in range(3)]
-                return jnp.concatenate(parts, axis=1)
-
-            both = jnp.dot(lines(taps_high), conv_both[...], preferred_element_type=F32)
-            low = jnp.dot(lines(taps_low), conv_both[:, 0:chan], preferred_element_type=F32)
-            total = both[:, 0:chan] + (both[:, chan:] + low)
-            conv_sum[pl.ds(n * step, step)] = total.reshape(step, cols, chan)
-            return 0
-
-        lax.fori_loop(0, rows // step, one, 0)
+            conv_sum[pl.ds(n * STEP, STEP)] = convolve(n)
+            return 0
+
+        lax.fori_loop(start, stop, one, 0)
 
     def read_out(r):
         def one(k, _):
@@ -344,7 +354,7 @@
             for q in range(BS):
                 spread[b, pl.ds(q, block_cols, stride=BS), :] = part
 
-    def combine(r, last):
+    def embed_inputs(r):
         wide = jnp.where(
             lax.broadcasted_iota(jnp.int32, (block_cols, cols), 1) // BS
             == lax.broadcasted_iota(jnp.int32, (block_cols, cols), 0), 1.0, 0.0).astype(BF16)
@@ -357,29 +367,44 @@
                 one_hot = jnp.where(
                     feature < 3, gone,
                     jnp.where(feature < 6, (1.0 - gone) * bits, (1.0 - gone) * (1.0 - bits))).astype(BF16)
-                inputs = lax.dot_general(
+                inputs[r, i] = lax.dot_general(
                     one_hot, embed, (((0,), (0,)), ((), ())), preferred_element_type=F32)
-                old = padded[1 + i, LEFT:LEFT + cols, :]
-                new = 0.5 * old + jnp.tanh(conv_sum[i] + inputs + spread[b])
-                if last:
-                    out_ref[i] = new
-                else:
-                    padded[1 + i, LEFT:LEFT + cols, :] = new
+
+    def updated(r, b, conv):
+        old = padded[pl.ds(1 + b * BS, BS), LEFT:LEFT + cols, :]
+        return 0.5 * old + jnp.tanh(conv + inputs[r, pl.ds(b * BS, BS)] + spread[b][None])
+
+    def combine(r):
+        def one(b, _):
+            new = updated(r, b, conv_sum[pl.ds(b * BS, BS)])
+            padded[pl.ds(1 + b * BS, BS), LEFT:LEFT + cols, :] = new
+            return 0
+
+        lax.fori_loop(0, block_rows, one, 0)
+
+    def store_out(n):
+        lines = pl.ds(n * STEP, STEP)
+        return pltpu.make_async_copy(conv_sum.at[lines], out_ref.at[lines], local_sem.at[3 + n])
+
+    chunks = rows // STEP
 
     build_cells()
     for_sides(lambda side: halo_arrival(0, side).wait_recv())
     place_borders(0)
     build_taps()
     next_wave(0)
-    convolve()
+    convolve_lines(0, chunks)
     next_wave(1)
+    embed_inputs(0)
+    embed_inputs(1)
     next_wave(2)
-    for wave in range(3):
-        for _, _, _, back in waves[wave]:
-            back.wait_recv()
+    for order in waves:
+        for wave in range(3):
+            for _, _, _, back in order[wave]:
+                back.wait_recv()
     own_in.wait_recv()
     read_out(0)
-    combine(0, False)
+    combine(0)
     pack_borders(1)
     for_sides(lambda side: halo_copy(1, side).start())
     build_cells()
@@ -387,13 +412,19 @@
     for_sides(lambda side: halo_arrival(1, side).wait_recv())
     place_borders(1)
     build_taps()
-    convolve()
-    combine(1, True)
-
-    for wave in range(3):
-        for out, _, on, _ in waves[wave]:
-            out.wait_send()
-            on.wait_send()
+    for n in range(chunks):
+        conv_sum[n * STEP:(n + 1) * STEP] = convolve(n)
+        for b in range(n * STEP // BS, (n + 1) * STEP // BS):
+            conv_sum[b * BS:(b + 1) * BS] = updated(1, b, conv_sum[b * BS:(b + 1) * BS])
+        store_out(n).start()
+
+    for order in waves:
+        for wave in range(3):
+            for out, _, on, _ in order[wave]:
+                out.wait_send()
+                on.wait_send()
+    for n in range(chunks):
+        store_out(n).wait()
     own_out.wait_send()
     for r in range(ROUNDS):
         for_sides(lambda side: halo_copy(r, side).wait_send())
@@ -404,7 +435,7 @@
     nx = gy_count // 2
     ny = nx
     nz = gx_count // ny
-    copies = 2 * max(nz - 1, ny - 1, nx - 1)
+    copies = max(nz - 1, ny - 1, nx - 1)
 
     def per_device(state, syndromes, erased, readers, conv, table, vector, read, offset):
         rows, cols, chan = state.shape
@@ -415,8 +446,8 @@
         return pl.pallas_call(
             functools.partial(kernel, (nz, ny, nx)),
             out_shape=jax.ShapeDtypeStruct(state.shape, F32),
-            in_specs=[pl.BlockSpec(memory_space=vmem)] * 9,
-            out_specs=pl.BlockSpec(memory_space=vmem),
+            in_specs=[pl.BlockSpec(memory_space=m) for m in (pl.ANY, vmem, vmem, vmem, pl.ANY, vmem, vmem, pl.ANY, vmem)],
+            out_specs=pl.BlockSpec(memory_space=pl.ANY),
             scratch_shapes=[
                 vmem((nz, ny, nx, 2, chan, chan), F32),
                 vmem((rows + 2, cols + 16, chan), F32),
@@ -436,17 +467,20 @@
                 vmem((ROUNDS, 2, rows, chan), F32),
                 vmem((ROUNDS, 4, 8, chan), F32),
                 vmem((ROUNDS, 4, 8, chan), F32),
-                dma((3, copies)),
-                dma((3, copies)),
-                dma((4, copies)),
-                dma((4, copies)),
+                vmem((9, chan, chan), F32),
+                vmem((ROUNDS, rows, cols, chan), F32),
+                dma((3 + rows // STEP,)),
+                dma((3, len(ORDERS), copies)),
+                dma((3, len(ORDERS), copies)),
+                dma((4, len(ORDERS), copies)),
+                dma((4, len(ORDERS), copies)),
                 dma((ROUNDS, 8)),
                 dma((ROUNDS, 8)),
             ],
             compiler_params=pltpu.CompilerParams(
                 collective_id=0, has_side_effects=True, vmem_limit_bytes=56 * 2**20
             ),
-        )(state, syndromes, erased, readers, conv, table, vector.reshape(1, -1), read, offset.reshape(1, -1))
+        )(state, syndromes, erased, readers.reshape(1, -1), conv, table, vector.reshape(1, -1), read, offset.reshape(1, -1))
 
     placed = (
         P("gx", "gy", None),

time: 46.6 us -> 39.9 us (0.86)
  Pallas kernels: 42.3 us -> 37.3 us
  local copies, waits for them, and re-layouts: 3.7 us -> 2.31 us
    pallas_call x1, Pallas kernels: 42.3 us -> 37.3 us  [per_device(): pl.pallas_call(functools.partial(kernel, (nz, ny, nx)), out_shape=jax.Sha...]
    unnamed x4 -> x1, local copies, waits for them, and re-layouts: 3.7 us -> 2.31 us
where the time goes in v2:
time: 39.9 us; the launch traced here: 39.7 us
  Pallas kernels  37.3 us (93%)
  local copies, waits for them, and re-layouts  2.31 us (6%)
    pallas_call x1, Pallas kernels, per_device(): pl.pallas_call(functools.partial(kernel, (nz, ny, nx)), out_shape=jax.Sha...  37.3 us
    unnamed x1, local copies, waits for them, and re-layouts  2.31 us

profile of v2, /device:TPU:1, one launch (start us, length us, event | category | flops | bytes accessed | tf_op | source)
XLA Modules:
  0.0 39.7 jit_solution(17375711365240376295)
XLA Ops:
  0.0 37.3 %shard_map.91 = f32[32,64,128]{2,1,0:T(8,128)} custom-call(f32[32,64,128]{2,1,0:T(8,128)} %state_ref.1, s32[2,32,64]{2,1,0:T(8,128)} %syn_ref.1, s32[2,8,16]{2,1,0:T(8,128)} %er_ref.1, s32[1,128]{1,0:T(1,128)} %bitcast.3, f32[9,128,128]{2,1,0:T(8,128)} %conv_ref.1, f32[2,128]{1,0:T(2,128)} %table_ref.1, f32[1,128]{1,0:T(1,128)} %bitcast.4, ...), custom_call_target="tpu_custom_call" | custom-call | tf_op jit(solution)/shard_map/pallas_call | solution.py:446
  37.4 2.3 %copy.11 = f32[32,64,128]{2,1,0:T(8,128)} copy(f32[32,64,128]{2,1,0:T(8,128)} %shard_map.91) | data formatting | bytes 2097152

commit v3 on v2

--- a/solution.py
+++ b/solution.py
@@ -291,13 +291,13 @@
                     cells[i * BS + q, pl.ds(b * block_cols, block_cols), chan:2 * chan] = low
             return 0
 
-        lax.fori_loop(0, block_rows, one, 0)
+        lax.fori_loop(0, block_rows, one, 0, unroll=2)
 
         def sort(p, _):
             sorted_cells[p] = jnp.dot(pick[...], cells[p], preferred_element_type=F32)
             return 0
 
-        lax.fori_loop(0, BS * BS, sort, 0)
+        lax.fori_loop(0, BS * BS, sort, 0, unroll=4)
 
     def build_taps():
         def one(i, _):
@@ -341,7 +341,7 @@
             pooled[pl.ds(pl.multiple_of(k * SLOTS, SLOTS), SLOTS), :] = mean
             return 0
 
-        lax.fori_loop(0, nz * ny * nx * 2, one, 0, unroll=4)
+        lax.fori_loop(0, nz * ny * nx * 2, one, 0, unroll=16)
         high, low = split_2(pooled[...])
         both = jnp.dot(place[...], jnp.concatenate([high, low], axis=1), preferred_element_type=F32)
         mean = both[:, 0:chan] + both[:, chan:]
@@ -380,7 +380,7 @@
             padded[pl.ds(1 + b * BS, BS), LEFT:LEFT + cols, :] = new
             return 0
 
-        lax.fori_loop(0, block_rows, one, 0)
+        lax.fori_loop(0, block_rows, one, 0, unroll=2)
 
     def store_out(n):
         lines = pl.ds(n * STEP, STEP)
@@ -389,12 +389,13 @@
     chunks = rows // STEP
 
     build_cells()
+    next_wave(0)
     for_sides(lambda side: halo_arrival(0, side).wait_recv())
     place_borders(0)
     build_taps()
-    next_wave(0)
-    convolve_lines(0, chunks)
+    convolve_lines(0, 2)
     next_wave(1)
+    convolve_lines(2, chunks)
     embed_inputs(0)
     embed_inputs(1)
     next_wave(2)

time: 39.9 us -> 35.8 us (0.90)
  Pallas kernels: 37.3 us -> 33.3 us
    pallas_call x1, Pallas kernels: 37.3 us -> 33.3 us  [per_device(): pl.pallas_call(functools.partial(kernel, (nz, ny, nx)), out_shape=jax.Sha...]
where the time goes in v3:
time: 35.8 us; the launch traced here: 35.6 us
  Pallas kernels  33.3 us (93%)
  local copies, waits for them, and re-layouts  2.31 us (6%)
    pallas_call x1, Pallas kernels, per_device(): pl.pallas_call(functools.partial(kernel, (nz, ny, nx)), out_shape=jax.Sha...  33.3 us
    unnamed x1, local copies, waits for them, and re-layouts  2.31 us

profile of v3, /device:TPU:1, one launch (start us, length us, event | category | flops | bytes accessed | tf_op | source)
XLA Modules:
  0.0 35.6 jit_solution(38974161792010734)
XLA Ops:
  0.0 33.3 %shard_map.91 = f32[32,64,128]{2,1,0:T(8,128)} custom-call(f32[32,64,128]{2,1,0:T(8,128)} %state_ref.1, s32[2,32,64]{2,1,0:T(8,128)} %syn_ref.1, s32[2,8,16]{2,1,0:T(8,128)} %er_ref.1, s32[1,128]{1,0:T(1,128)} %bitcast.3, f32[9,128,128]{2,1,0:T(8,128)} %conv_ref.1, f32[2,128]{1,0:T(2,128)} %table_ref.1, f32[1,128]{1,0:T(1,128)} %bitcast.4, ...), custom_call_target="tpu_custom_call" | custom-call | tf_op jit(solution)/shard_map/pallas_call | solution.py:447
  33.3 2.3 %copy.11 = f32[32,64,128]{2,1,0:T(8,128)} copy(f32[32,64,128]{2,1,0:T(8,128)} %shard_map.91) | data formatting | bytes 2097152
